TPU v7x, 32 devices: a whole 2x2x4 slice. The times are simulated.
32 devices in a mesh: gx: 8 (over y, x, core), gy: 4 (over z).
Axes of the slice: x: 2, y: 2, z: 4, core: 2. Of those that a mesh axis runs over, the one named last changes fastest.
Arguments:
- queries: bfloat16 [1024, 256], P(('gx', 'gy')), may hold values from -32 to 32
- positions: int32 [1024], P(('gx', 'gy')), may hold values from 0 to 16383
- queue: bfloat16 [16384, 256], P('gx'), may hold values from -4 to 4
- new_keys: bfloat16 [2048, 256], P(('gx', 'gy')), may hold values from -4 to 4
- step: int32 [1], replicated, may hold values from 0 to 1023
Outputs:
- losses: float32 [1024], P(('gx', 'gy'))
- query_grad: bfloat16 [1024, 256], P(('gx', 'gy'))
- updated_queue: bfloat16 [16384, 256], P('gx')
All inputs are finite; a program needn't handle non-finite values.
Results may differ from a plain program's by a relative error of at most 0.0029.
Values may be sent and summed in bfloat16 or wider, within the bound.
A program may use at most 64 MiB of HBM per device.

v0:
```python
import math

import jax
import jax.numpy as jnp
from jax import lax
from jax.sharding import PartitionSpec as P


def local(queries, positions, queue, new_keys, step):
    q_dev = queries.shape[0]
    key_dev = queue.shape[0]
    width = queue.shape[1]
    scale = 2.0 / math.sqrt(width)
    slab_count = lax.axis_size("gx")
    slab_index = lax.axis_index("gx")
    all_rows, all_targets = (
        lax.all_gather(queries, "gx", axis=0, tiled=True),
        lax.all_gather(positions, "gx", axis=0, tiled=True),
    )
    arrived = lax.all_gather(new_keys, ("gx", "gy"), axis=0, tiled=True)
    scores = jnp.einsum("re,ke->rk", all_rows, queue, preferred_element_type=jnp.float32) * scale
    local_target = all_targets - slab_index * key_dev
    hits = lax.broadcasted_iota(jnp.int32, scores.shape, 1) == local_target[:, None]
    positive = jnp.sum(jnp.where(hits, scores, 0.0), axis=1)
    top = jnp.max(scores, axis=1)
    total = jnp.sum(jnp.exp(scores - top[:, None]), axis=1)
    top_all = lax.pmax(top, "gx")
    total_all, positive_all = lax.psum((total * jnp.exp(top - top_all), positive), "gx")
    lse = top_all + jnp.log(total_all)
    loss_rows = lse - positive_all
    losses = lax.dynamic_slice_in_dim(loss_rows, slab_index * q_dev, q_dev, 0)
    weights = (jnp.exp(scores - lse[:, None]) - hits.astype(jnp.float32)).astype(jnp.bfloat16)
    partial_grad = jnp.dot(weights, queue, preferred_element_type=jnp.float32)
    full_grad = lax.psum(partial_grad, "gx")
    summed = lax.dynamic_slice_in_dim(full_grad, slab_index * q_dev, q_dev, 0)
    query_grad = (summed * scale).astype(jnp.bfloat16)
    owner = step[0] % slab_count
    updated_queue = jnp.where(owner == slab_index, arrived, queue)
    return (losses, query_grad, updated_queue)


def solution(mesh):
    return jax.shard_map(
        local,
        mesh=mesh,
        in_specs=(
            P(("gx", "gy"), None),
            P(("gx", "gy")),
            P("gx", None),
            P(("gx", "gy"), None),
            P(),
        ),
        out_specs=(P(("gx", "gy")), P(("gx", "gy"), None), P("gx", None)),
        check_vma=False,
    )
```

profile of v0, /device:TPU:0, one launch (start us, length us, event | category | flops | bytes accessed | tf_op | source)
XLA Modules:
  0.0 122.9 jit_solution(12722619993717123457)
XLA Ops:
  8.0 0.0 all-reduce.4.cloned.1.call-start
  8.0 10.8 %all_gather.9 = bf16[256,256]{1,0:T(8,128)(2,1)S(1)} all-gather(bf16[32,256]{1,0:T(8,128)(2,1)} %param.5), channel_id=1, replica_groups=mesh['gx'=8,'gy'=4] {'gx'}, dimensions={0}, use_global_device_ids=true | all-gather | bytes 147456 | tf_op jit(solution)/shard_map/all_gather | solution.py:17
  18.9 1.2 %dynamic-slice = u32[1]{0:T(128)} dynamic-slice(u32[32]{0:T(128)} %constant.35, u32[]{:T(128)S(6)} %add.20), dynamic_slice_sizes={1} | dynamic-slice | bytes 12
  20.8 0.9 dynamic-update-slice
  21.7 7.2 %all-reduce = s32[256]{0:T(256)S(1)} all-reduce(s32[256]{0:T(256)S(1)} %dynamic-update-slice), channel_id=1, replica_groups=mesh['gx'=8,'gy'=4] {'gx'}, use_global_device_ids=true, to_apply=%add | all-reduce | flops 256 | bytes 2048
  28.8 0.0 copy-start
  28.8 1.9 %fusion.4 = (f32[256]{0:T(256)S(1)}, f32[256,2048]{1,0:T(8,128)S(1)}) fusion(bf16[256,256]{1,0:T(8,128)(2,1)S(1)} %all_gather.9, bf16[2048,256]{1,0:T(8,128)(2,1)} %param.7), kind=kOutput, calls=%fused_computation.14 | convolution fusion | flops 269483776 | bytes 3277824 | tf_op jit(solution)/shard_map/re,ke->rk/dot_general | solution.py:21
  30.7 11.8 %pmax.7 = f32[256]{0:T(256)S(1)} all-reduce(f32[256]{0:T(256)S(1)} %get-tuple-element.9), channel_id=1, replica_groups=mesh['gx'=8,'gy'=4] {'gx'}, use_global_device_ids=true, to_apply=%region_1.2 | all-reduce | flops 256 | bytes 2048 | tf_op jit(solution)/shard_map/pmax | solution.py:27
  42.5 0.8 select_reduce_fusion
  43.3 11.8 %all-reduce.1 = (f32[256]{0:T(256)S(1)}, f32[256]{0:T(256)S(1)}) all-reduce(f32[256]{0:T(256)S(1)} %exponential_multiply_fusion, f32[256]{0:T(256)S(1)} %get-tuple-element.3), channel_id=1, replica_groups=mesh['gx'=8,'gy'=4] {'gx'}, use_global_device_ids=true, to_apply=%region_3.4 | all-reduce | flops 512 | bytes 4096 | tf_op jit(solution)/shard_map/psum | solution.py:28
  55.1 0.0 copy-done
  55.1 1.4 %fusion = f32[256,256]{1,0:T(8,128)} fusion(bf16[2048,256]{1,0:T(8,128)(2,1)S(1)} %copy-done, f32[256,2048]{1,0:T(8,128)S(1)} %get-tuple-element.10, f32[256]{0:T(256)S(1)} %get-tuple-element.8, s32[256]{0:T(256)S(1)} %broadcast_subtract_fusion), kind=kOutput, calls=%fused_computation.5 | convolution fusion | flops 271056896 | bytes 3409920 | tf_op jit(solution)/shard_map/dot_general | solution.py:33
  56.5 0.0 all-reduce.4.cloned.1.call-update
  56.5 0.0 all-gather.2.cloned.1.call-start
  56.5 0.5 all-gather.2.cloned.1.call-update
  57.7 0.6 dynamic_slice.6
  58.3 53.1 %all-reduce.4.cloned.1.call-done = f32[256,256]{1,0:T(8,128)} async-done(((f32[256,256]{1,0:T(8,128)}), f32[256,256]{1,0:T(8,128)}) %all-reduce.4.cloned.1.call-update) | async-done | bytes 262160 | tf_op jit(solution)/shard_map/psum | solution.py:34
  111.4 1.4 %multiply_convert_fusion = bf16[32,256]{1,0:T(8,128)(2,1)} fusion(f32[256,256]{1,0:T(8,128)} %all-reduce.4.cloned.1.call-done, s32[]{:T(128)S(6)} %select_n.24), kind=kLoop, calls=%fused_computation.9 | loop fusion | flops 16384 | bytes 49156 | tf_op jit(solution)/shard_map/convert_element_type | solution.py:36
  112.8 1.6 %all-gather.2.cloned.1.call-done = bf16[2048,256]{1,0:T(8,128)(2,1)} async-done(((bf16[64,256]{1,0:T(8,128)(2,1)}), bf16[2048,256]{1,0:T(8,128)(2,1)}) %all-gather.2.cloned.1.call-update) | async-done | bytes 1048592 | tf_op jit(solution)/shard_map/all_gather | solution.py:20
  114.4 1.1 broadcast_select_fusion
  (4 shorter events, 0.0 us)
Async XLA Ops:
  8.0 103.4 %all-reduce.4.cloned.1.call-start = ((), (), s32[]{:S(2)}) async-start(), calls=%async_computation | async-start | bytes 524288 | tf_op jit(solution)/shard_map/psum | solution.py:34
  28.8 26.3 %copy-start = (bf16[2048,256]{1,0:T(8,128)(2,1)S(1)}, bf16[2048,256]{1,0:T(8,128)(2,1)}, u32[]{:S(2)}) copy-start(bf16[2048,256]{1,0:T(8,128)(2,1)} %param.7) | copy-start | bytes 3145732
  56.5 57.9 %all-gather.2.cloned.1.call-start = ((), (), s32[]{:S(2)}) async-start(), calls=%async_computation.1 | async-start | bytes 1081344 | tf_op jit(solution)/shard_map/all_gather | solution.py:20
Sparse Core Ops, SparseCore 0:
  56.6 54.7 all-reduce.3
Sparse Core Ops, SparseCore 1:
  60.4 53.9 all-gather.1
where the time goes:
time: 124 us; the launch traced here: 123 us
  waiting for transfers between devices  55.2 us (45%)
  blocking collectives  41.6 us (34%)
  between operations  16.8 us (14%)
  matrix products  3.25 us (3%)
  other arithmetic  3.23 us (3%)
  local copies, waits for them, and re-layouts  2.69 us (2%)
    psum x1, waiting for transfers between devices, local(): full_grad = lax.psum(partial_grad, 'gx')  53.1 us
    psum x1, blocking collectives, local(): lax.psum((total * jnp.exp(top - top_all), positive), 'gx')  11.8 us
    pmax x1, blocking collectives, local(): top_all = lax.pmax(top, 'gx')  11.8 us
    all_gather x1, blocking collectives, local(): lax.all_gather(queries, 'gx', axis=0, tiled=True)  10.8 us
    unnamed x1, blocking collectives  7.17 us
  transfers between devices with their start and end apart: 2, of which 2 were waited for; matrix products, arithmetic and copies ran while one was open for 2% of the time, Pallas kernels for 0%

commit v1 on v0

v1 whole, which is shorter than its diff:
```python
import functools
import math

import jax
import jax.numpy as jnp
from jax import lax
from jax.experimental import pallas as pl
from jax.experimental.pallas import tpu as pltpu
from jax.sharding import PartitionSpec as P

MESH = pl.DeviceIdType.MESH
LANES = 128
F32 = jnp.float32
BF16 = jnp.bfloat16


def diagonal(rows):
    shape = (rows, LANES)
    return lax.broadcasted_iota(jnp.int32, shape, 0) == lax.broadcasted_iota(jnp.int32, shape, 1)


def to_column(row, diag):
    return jnp.sum(jnp.where(diag, row, 0.0), axis=1, keepdims=True)


def to_row(column, diag):
    return jnp.sum(jnp.where(diag, column, 0.0), axis=0, keepdims=True)


def exchange(
    n, ngy, scale,
    q_ref, pos_ref, queue_ref, nk_ref,
    loss_ref, grad_ref, arrived_ref,
    keys, q_all, p_all, pos_v, part_send, part_recv, stat_send, stat_recv,
    local_sem, q_ss, q_rs, p_ss, p_rs, z_ss, z_rs, k_ss, f_ss, k_rs, g_ss, g_rs, s_ss, s_rs,
):
    i = lax.axis_index("gx")
    j = lax.axis_index("gy")
    q_dev, width = q_ref.shape
    key_dev = queue_ref.shape[0]

    def send(src, dst, ss, rs, to):
        return pltpu.make_async_remote_copy(
            src_ref=src, dst_ref=dst, send_sem=ss, recv_sem=rs, device_id=to, device_id_type=MESH
        )

    def gx_peers(body):
        for d in range(1, n):
            body(lax.rem(i + d, n))

    def gy_peers(body):
        for d in range(1, ngy):
            body(lax.rem(j + d, ngy))

    load_pos = pltpu.make_async_copy(pos_ref, pos_v, local_sem.at[0])
    load_q = pltpu.make_async_copy(q_ref, q_all.at[i], local_sem.at[1])
    load_keys = pltpu.make_async_copy(queue_ref, keys, local_sem.at[2])
    own_new = pltpu.make_async_copy(nk_ref, arrived_ref.at[i * ngy + j], local_sem.at[3])
    load_pos.start()
    load_q.start()
    load_keys.start()
    own_new.start()

    barrier = pltpu.get_barrier_semaphore()
    gx_peers(lambda p: pl.semaphore_signal(barrier, inc=1, device_id=(p, j), device_id_type=MESH))
    gy_peers(lambda p: pl.semaphore_signal(barrier, inc=1, device_id=(i, p), device_id_type=MESH))
    load_pos.wait()
    load_q.wait()
    diag = diagonal(q_dev)
    p_all[i] = jnp.zeros((1, LANES), jnp.int32)
    p_all[i, :, 0:q_dev] = pos_v[...].reshape(1, q_dev)
    pl.semaphore_wait(barrier, n + ngy - 2)

    def q_copy(p):
        return send(q_all.at[i], q_all.at[i], q_ss.at[p], q_rs.at[i], (p, j))

    def p_copy(p):
        return send(p_all.at[i], p_all.at[i], p_ss.at[p], p_rs.at[i], (p, j))

    def start_queries(p):
        p_copy(p).start()
        q_copy(p).start()

    gx_peers(start_queries)

    def z_copy(p):
        return send(nk_ref, arrived_ref.at[i * ngy + j], z_ss.at[p], z_rs.at[j], (i, p))

    gy_peers(lambda p: z_copy(p).start())

    def wait_in(dst, sem):
        pltpu.make_async_copy(dst, dst, sem).wait()

    partner = i + 1 - 2 * lax.rem(i, 2)

    def rows_of(k):
        return arrived_ref.at[pl.ds(k * ngy, ngy)]

    def k_copy(p):
        return send(rows_of(i), rows_of(i), k_ss.at[p], k_rs.at[i], (p, j))

    def f_copy(k):
        return send(rows_of(k), rows_of(k), f_ss.at[k], k_rs.at[k], (partner, j))

    def same_core(body):
        for d in range(2, n, 2):
            body(lax.rem(i + d, n))

    load_keys.wait()

    def wait_queries(p):
        wait_in(p_all.at[p], p_rs.at[p])
        wait_in(q_all.at[p], q_rs.at[p])

    gx_peers(wait_queries)

    own_new.wait()
    gy_peers(lambda p: wait_in(arrived_ref.at[i * ngy + p], z_rs.at[p]))
    same_core(lambda p: k_copy(p).start())
    k_copy(partner).start()

    group = min(n, 256 // q_dev)
    rows = group * q_dev

    def work(c):
        at = c * group
        columns = [to_column(p_all[at + b].astype(F32), diag) for b in range(group)]
        target = jnp.concatenate(columns, axis=0).astype(jnp.int32) - i * key_dev
        q = q_all[pl.ds(at, group)].reshape(rows, width)
        slab = keys[...]
        scores = lax.dot_general(q, slab, (((1,), (1,)), ((), ())), preferred_element_type=F32) * scale
        hits = lax.broadcasted_iota(jnp.int32, scores.shape, 1) == target
        top = jnp.max(scores, axis=1, keepdims=True)
        positive = jnp.sum(jnp.where(hits, scores, 0.0), axis=1, keepdims=True)
        powers = jnp.exp(scores - top)
        total = jnp.sum(powers, axis=1, keepdims=True)
        others = jnp.where(hits, 0.0, powers).astype(BF16)
        part = jnp.dot(others, slab, preferred_element_type=F32)
        row = jnp.dot(hits.astype(F32).astype(BF16), slab, preferred_element_type=F32)
        high = part.astype(BF16)
        low = part - high.astype(F32)
        inside = jnp.logical_and(target >= 0, target < key_dev)
        second = jnp.where(inside, row, low).astype(BF16)
        part_send[pl.ds(at, group), 0] = high.reshape(group, q_dev, width)
        part_send[pl.ds(at, group), 1] = second.reshape(group, q_dev, width)
        for b in range(group):
            span = slice(b * q_dev, (b + 1) * q_dev)
            stat_send[at + b, 0:1] = to_row(top[span], diag)
            stat_send[at + b, 1:2] = to_row(total[span], diag)
            stat_send[at + b, 2:3] = to_row(positive[span], diag)
            stat_send[at + b, 3:4] = jnp.zeros((1, LANES), F32)

    if n == group:
        work(0)
    else:
        pl.loop(0, n // group)(work)

    def g_copy(p):
        return send(part_send.at[p], part_recv.at[i], g_ss.at[p], g_rs.at[i], (p, j))

    def s_copy(p):
        return send(stat_send.at[p], stat_recv.at[i], s_ss.at[p], s_rs.at[i], (p, j))

    def start_parts(p):
        s_copy(p).start()
        g_copy(p).start()

    gx_peers(start_parts)
    part_recv[i] = part_send[i]
    stat_recv[i] = stat_send[i]

    def pass_on(k):
        wait_in(rows_of(k), k_rs.at[k])
        f_copy(k).start()

    same_core(pass_on)

    gx_peers(lambda p: wait_in(stat_recv.at[p], s_rs.at[p]))
    top = stat_recv[0, 0:1]
    for s in range(1, n):
        top = jnp.maximum(top, stat_recv[s, 0:1])
    total = jnp.zeros_like(top)
    positive = jnp.zeros_like(top)
    for s in range(n):
        total = total + stat_recv[s, 1:2] * jnp.exp(stat_recv[s, 0:1] - top)
        positive = positive + stat_recv[s, 2:3]
    lse = top + jnp.log(total)
    loss_ref[...] = lse - positive
    own = to_column(p_all[i].astype(F32), diag).astype(jnp.int32)
    at_positive = to_column(jnp.exp(positive - lse) - 1.0, diag)
    factors = [to_column(jnp.exp(stat_recv[s, 0:1] - lse), diag) for s in range(n)]

    gx_peers(lambda p: wait_in(part_recv.at[p], g_rs.at[p]))
    grad = jnp.zeros((q_dev, width), F32)
    for s in range(n):
        first = part_recv[s, 0].astype(F32)
        second = part_recv[s, 1].astype(F32)
        inside = jnp.logical_and(own >= s * key_dev, own < (s + 1) * key_dev)
        grad = grad + factors[s] * first + jnp.where(inside, at_positive, factors[s]) * second
    grad_ref[...] = (grad * scale).astype(BF16)

    wait_in(rows_of(partner), k_rs.at[partner])
    for d in range(2, n, 2):
        k = lax.rem(partner + d, n)
        wait_in(rows_of(k), k_rs.at[k])

    def end_sends(p):
        p_copy(p).wait_send()
        q_copy(p).wait_send()
        s_copy(p).wait_send()
        g_copy(p).wait_send()

    gx_peers(end_sends)
    gy_peers(lambda p: z_copy(p).wait_send())
    same_core(lambda p: k_copy(p).wait_send())
    k_copy(partner).wait_send()
    same_core(lambda k: f_copy(k).wait_send())


def finish(
    n, step_ref, loss_ref, grad_ref, queue_ref, arrived_ref, loss_out, grad_out, updated_ref, sem
):
    here = lax.rem(step_ref[0], n) == lax.axis_index("gx")

    @pl.when(here)
    def _():
        pltpu.make_async_copy(arrived_ref, updated_ref, sem.at[0]).start()

    @pl.when(jnp.logical_not(here))
    def _():
        pltpu.make_async_copy(queue_ref, updated_ref, sem.at[0]).start()

    loss_out[...] = loss_ref[0, 0 : loss_out.shape[0]]
    grad_out[...] = grad_ref[...]
    pltpu.make_async_copy(queue_ref, updated_ref, sem.at[0]).wait()


def local(n, ngy, queries, positions, queue, new_keys, step):
    q_dev, width = queries.shape
    key_dev = queue.shape[0]
    nk_dev = new_keys.shape[0]
    scale = 2.0 / math.sqrt(width)
    anywhere = pl.BlockSpec(memory_space=pl.ANY)
    vmem = pl.BlockSpec(memory_space=pltpu.VMEM)
    dma = pltpu.SemaphoreType.DMA
    rows = n * q_dev
    loss_row, grad, arrived = pl.pallas_call(
        functools.partial(exchange, n, ngy, scale),
        out_shape=(
            jax.ShapeDtypeStruct((1, LANES), F32),
            jax.ShapeDtypeStruct((q_dev, width), BF16),
            jax.ShapeDtypeStruct((n * ngy, nk_dev, width), BF16),
        ),
        in_specs=[anywhere] * 4,
        out_specs=(vmem, vmem, anywhere),
        scratch_shapes=[
            pltpu.VMEM((key_dev, width), BF16),
            pltpu.VMEM((n, q_dev, width), BF16),
            pltpu.VMEM((n, 1, LANES), jnp.int32),
            pltpu.VMEM((q_dev,), jnp.int32),
            pltpu.VMEM((n, 2, q_dev, width), BF16),
            pltpu.VMEM((n, 2, q_dev, width), BF16),
            pltpu.VMEM((n, 4, LANES), F32),
            pltpu.VMEM((n, 4, LANES), F32),
            dma((4,)),
            dma((n,)), dma((n,)), dma((n,)), dma((n,)),
            dma((ngy,)), dma((ngy,)),
            dma((n,)), dma((n,)), dma((n,)),
            dma((n,)), dma((n,)), dma((n,)), dma((n,)),
        ],
        compiler_params=pltpu.CompilerParams(
            collective_id=0, has_side_effects=True, vmem_limit_bytes=48 * 2**20
        ),
        cost_estimate=pl.CostEstimate(
            flops=6 * rows * key_dev * width,
            bytes_accessed=2 * key_dev * width * 2,
            transcendentals=rows * key_dev,
        ),
        name="exchange",
    )(queries, positions, queue, new_keys)
    return pl.pallas_call(
        functools.partial(finish, n),
        out_shape=(
            jax.ShapeDtypeStruct((q_dev,), F32),
            jax.ShapeDtypeStruct((q_dev, width), BF16),
            jax.ShapeDtypeStruct((key_dev, width), BF16),
        ),
        in_specs=[pl.BlockSpec(memory_space=pltpu.SMEM), vmem, vmem, anywhere, anywhere],
        out_specs=(vmem, vmem, anywhere),
        scratch_shapes=[dma((1,))],
        name="finish",
    )(step, loss_row, grad, queue, arrived.reshape(key_dev, width))


def solution(mesh):
    return jax.shard_map(
        functools.partial(local, mesh.shape["gx"], mesh.shape["gy"]),
        mesh=mesh,
        in_specs=(
            P(("gx", "gy"), None),
            P(("gx", "gy")),
            P("gx", None),
            P(("gx", "gy"), None),
            P(),
        ),
        out_specs=(P(("gx", "gy")), P(("gx", "gy"), None), P("gx", None)),
        check_vma=False,
    )
```

time: 124 us -> 61.4 us (0.50)
  waiting for transfers between devices: 55.2 us -> 0 us
  Pallas kernels: 0 us -> 54.9 us
  blocking collectives: 41.6 us -> 0 us
  between operations: 16.8 us -> 1.33 us
  matrix products: 3.25 us -> 0 us
  other arithmetic: 3.23 us -> 0 us
  local copies, waits for them, and re-layouts: 2.69 us -> 4.78 us
    pallas_call x0 -> x2, Pallas kernels: none -> 54.9 us  [the longest x1 34.2 us: local(): pl.pallas_call(functools.partial(finish, n), out_shape=(jax.ShapeDtypeStr...]
    psum x1 -> x0, waiting for transfers between devices: 53.1 us -> none  [local(): full_grad = lax.psum(partial_grad, 'gx')]
    psum x1 -> x0, blocking collectives: 11.8 us -> none  [local(): lax.psum((total * jnp.exp(top - top_all), positive), 'gx')]
    pmax x1 -> x0, blocking collectives: 11.8 us -> none  [local(): top_all = lax.pmax(top, 'gx')]
    all_gather x1 -> x0, blocking collectives: 10.8 us -> none  [local(): lax.all_gather(queries, 'gx', axis=0, tiled=True)]
    unnamed x1 -> x0, blocking collectives: 7.17 us -> none
    dot_general x2 -> x0, matrix products: 3.25 us -> none  [the longest x1 1.86 us: local(): jnp.einsum('re,ke->rk', all_rows, queue, preferred_element_type=jnp.float32)]
    unnamed x5 -> x14, local copies, waits for them, and re-layouts: 2.1 us -> 4.78 us
  transfers between devices with their start and end apart: 2 -> 0, of which waited for: 2 -> 0; matrix products, arithmetic and copies ran while one was open for 2% -> 0% of each run, Pallas kernels for 0% -> 0%
where the time goes in v1:
time: 61.4 us; the launch traced here: 61 us
  Pallas kernels  54.9 us (89%)
  local copies, waits for them, and re-layouts  4.78 us (8%)
  between operations  1.33 us (2%)
    pallas_call x1, Pallas kernels, local(): pl.pallas_call(functools.partial(finish, n), out_shape=(jax.ShapeDtypeStr...  34.2 us
    pallas_call x1, Pallas kernels, local(): pl.pallas_call(functools.partial(exchange, n, ngy, scale), out_shape=(jax...  20.7 us
    unnamed x14, local copies, waits for them, and re-layouts  4.78 us

profile of v1, /device:TPU:0, one launch (start us, length us, event | category | flops | bytes accessed | tf_op | source)
XLA Modules:
  0.0 61.0 jit_solution(2329637103302578997)
XLA Ops:
  0.6 0.0 copy-start.6
  1.3 0.0 copy-done.6
  1.3 0.0 copy-start
  1.3 1.2 %copy-done = bf16[2048,256]{1,0:T(8,128)(2,1)S(1)} copy-done((bf16[2048,256]{1,0:T(8,128)(2,1)S(1)}, bf16[2048,256]{1,0:T(8,128)(2,1)}, u32[]{:S(2)}) %copy-start) | copy-done | bytes 1048600
  2.5 0.0 copy-start.4
  2.5 0.8 %copy-done.4 = bf16[64,256]{1,0:T(8,128)(2,1)S(1)} copy-done((bf16[64,256]{1,0:T(8,128)(2,1)S(1)}, bf16[64,256]{1,0:T(8,128)(2,1)}, u32[]{:S(2)}) %copy-start.4) | copy-done | bytes 32792
  3.3 0.0 copy-start.5
  3.3 0.7 %copy-done.5 = bf16[32,256]{1,0:T(8,128)(2,1)S(1)} copy-done((bf16[32,256]{1,0:T(8,128)(2,1)S(1)}, bf16[32,256]{1,0:T(8,128)(2,1)}, u32[]{:S(2)}) %copy-start.5) | copy-done | bytes 16408
  4.0 20.7 %exchange.1 = (f32[1,128]{1,0:T(1,128)S(1)}, bf16[32,256]{1,0:T(8,128)(2,1)S(1)}, bf16[32,64,256]{2,1,0:T(8,128)(2,1)S(1)}) custom-call(bf16[32,256]{1,0:T(8,128)(2,1)S(1)} %copy-done.5, s32[32]{0:T(128)S(1)} %copy-done.6, bf16[2048,256]{1,0:T(8,128)(2,1)S(1)} %copy-done, bf16[64,256]{1,0:T(8,128)(2,1)S(1)} %copy-done.4), custom_call_target="tpu_custom_call" | custom-call | flops 805306368 | bytes 2097152 | tf_op jit(solution)/shard_map/exchange/pallas_call | solution.py:247
  24.7 0.0 copy-start.1
  24.7 1.0 %copy-done.1 = bf16[32,64,256]{2,1,0:T(8,128)(2,1)} copy-done((bf16[32,64,256]{2,1,0:T(8,128)(2,1)}, bf16[32,64,256]{2,1,0:T(8,128)(2,1)S(1)}, u32[]{:S(2)}) %copy-start.1) | copy-done | bytes 1048600
  25.7 0.0 copy-start.2
  25.7 0.6 copy-done.2
  26.3 0.0 copy-start.3
  26.3 0.5 copy-done.3
  26.8 34.2 %finish.1 = (f32[32]{0:T(128)}, bf16[32,256]{1,0:T(8,128)(2,1)}, bf16[2048,256]{1,0:T(8,128)(2,1)}) custom-call(s32[1]{0:T(128)S(6)} %copy.8.step_ref, f32[1,128]{1,0:T(1,128)} %copy-done.3, bf16[32,256]{1,0:T(8,128)(2,1)} %copy-done.2, bf16[2048,256]{1,0:T(8,128)(2,1)} %queue_ref.3, bf16[2048,256]{1,0:T(8,128)(2,1)} %bitcast.1), custom_call_target="tpu_custom_call" | custom-call | tf_op jit(solution)/shard_map/finish/pallas_call | solution.py:281
Async XLA Ops:
  0.6 0.7 %copy-start.6 = (s32[32]{0:T(128)S(1)}, s32[32]{0:T(128)}, u32[]{:S(2)}) copy-start(s32[32]{0:T(128)} %pos_ref.1) | copy-start | bytes 388
  1.3 1.2 %copy-start = (bf16[2048,256]{1,0:T(8,128)(2,1)S(1)}, bf16[2048,256]{1,0:T(8,128)(2,1)}, u32[]{:S(2)}) copy-start(bf16[2048,256]{1,0:T(8,128)(2,1)} %queue_ref.3) | copy-start | bytes 3145732
  2.5 0.8 %copy-start.4 = (bf16[64,256]{1,0:T(8,128)(2,1)S(1)}, bf16[64,256]{1,0:T(8,128)(2,1)}, u32[]{:S(2)}) copy-start(bf16[64,256]{1,0:T(8,128)(2,1)} %nk_ref.1) | copy-start | bytes 98308
  3.3 0.7 %copy-start.5 = (bf16[32,256]{1,0:T(8,128)(2,1)S(1)}, bf16[32,256]{1,0:T(8,128)(2,1)}, u32[]{:S(2)}) copy-start(bf16[32,256]{1,0:T(8,128)(2,1)} %q_ref.1) | copy-start | bytes 49156
  24.7 1.0 %copy-start.1 = (bf16[32,64,256]{2,1,0:T(8,128)(2,1)}, bf16[32,64,256]{2,1,0:T(8,128)(2,1)S(1)}, u32[]{:S(2)}) copy-start(bf16[32,64,256]{2,1,0:T(8,128)(2,1)S(1)} %get-tuple-element.8) | copy-start | bytes 3145732
  25.7 0.6 copy-start.2
  26.3 0.5 copy-start.3

commit v2 on v1

--- a/solution.py
+++ b/solution.py
@@ -30,8 +30,8 @@
 def exchange(
     n, ngy, scale,
     q_ref, pos_ref, queue_ref, nk_ref,
-    loss_ref, grad_ref, arrived_ref,
-    keys, q_all, p_all, pos_v, part_send, part_recv, stat_send, stat_recv,
+    loss_ref, grad_ref, gathered_ref,
+    arrived_ref, keep_sem, keys, q_all, p_all, pos_v, part_send, part_recv, stat_send, stat_recv,
     local_sem, q_ss, q_rs, p_ss, p_rs, z_ss, z_rs, k_ss, f_ss, k_rs, g_ss, g_rs, s_ss, s_rs,
 ):
     i = lax.axis_index("gx")
@@ -84,8 +84,9 @@
     gx_peers(start_queries)
 
     def z_copy(p):
-        return send(nk_ref, arrived_ref.at[i * ngy + j], z_ss.at[p], z_rs.at[j], (i, p))
-
+        return send(arrived_ref.at[i * ngy + j], arrived_ref.at[i * ngy + j], z_ss.at[p], z_rs.at[j], (i, p))
+
+    own_new.wait()
     gy_peers(lambda p: z_copy(p).start())
 
     def wait_in(dst, sem):
@@ -114,10 +115,14 @@
 
     gx_peers(wait_queries)
 
-    own_new.wait()
     gy_peers(lambda p: wait_in(arrived_ref.at[i * ngy + p], z_rs.at[p]))
     same_core(lambda p: k_copy(p).start())
     k_copy(partner).start()
+
+    def keep(k):
+        return pltpu.make_async_copy(rows_of(k), gathered_ref.at[pl.ds(k * ngy, ngy)], keep_sem.at[k])
+
+    keep(i).start()
 
     group = min(n, 256 // q_dev)
     rows = group * q_dev
@@ -172,6 +177,7 @@
     def pass_on(k):
         wait_in(rows_of(k), k_rs.at[k])
         f_copy(k).start()
+        keep(k).start()
 
     same_core(pass_on)
 
@@ -199,10 +205,10 @@
         grad = grad + factors[s] * first + jnp.where(inside, at_positive, factors[s]) * second
     grad_ref[...] = (grad * scale).astype(BF16)
 
-    wait_in(rows_of(partner), k_rs.at[partner])
-    for d in range(2, n, 2):
+    for d in range(0, n, 2):
         k = lax.rem(partner + d, n)
         wait_in(rows_of(k), k_rs.at[k])
+        keep(k).start()
 
     def end_sends(p):
         p_copy(p).wait_send()
@@ -215,24 +221,55 @@
     same_core(lambda p: k_copy(p).wait_send())
     k_copy(partner).wait_send()
     same_core(lambda k: f_copy(k).wait_send())
+    for k in range(n):
+        keep(k).wait()
 
 
 def finish(
-    n, step_ref, loss_ref, grad_ref, queue_ref, arrived_ref, loss_out, grad_out, updated_ref, sem
+    n, step_ref, loss_ref, grad_ref, queue_ref, arrived_ref, loss_out, grad_out, updated_ref,
+    loss_v, loss_w, grad_v, slab, in_sem, out_sem, small_in, small_out,
 ):
     here = lax.rem(step_ref[0], n) == lax.axis_index("gx")
+    pieces = in_sem.shape[0]
+    size = slab.shape[0] // pieces
+
+    def part(c):
+        return pl.ds(c * size, size)
+
+    def load(src, c):
+        return pltpu.make_async_copy(src.at[part(c)], slab.at[part(c)], in_sem.at[c])
+
+    def store(c):
+        return pltpu.make_async_copy(slab.at[part(c)], updated_ref.at[part(c)], out_sem.at[c])
 
     @pl.when(here)
     def _():
-        pltpu.make_async_copy(arrived_ref, updated_ref, sem.at[0]).start()
+        for c in range(pieces):
+            load(arrived_ref, c).start()
 
     @pl.when(jnp.logical_not(here))
     def _():
-        pltpu.make_async_copy(queue_ref, updated_ref, sem.at[0]).start()
-
-    loss_out[...] = loss_ref[0, 0 : loss_out.shape[0]]
-    grad_out[...] = grad_ref[...]
-    pltpu.make_async_copy(queue_ref, updated_ref, sem.at[0]).wait()
+        for c in range(pieces):
+            load(queue_ref, c).start()
+
+    loss_load = pltpu.make_async_copy(loss_ref, loss_v, small_in.at[0])
+    grad_load = pltpu.make_async_copy(grad_ref, grad_v, small_in.at[1])
+    loss_store = pltpu.make_async_copy(loss_w, loss_out, small_out.at[0])
+    grad_store = pltpu.make_async_copy(grad_v, grad_out, small_out.at[1])
+    loss_load.start()
+    grad_load.start()
+    for c in range(pieces):
+        load(queue_ref, c).wait()
+        store(c).start()
+    loss_load.wait()
+    loss_w[...] = loss_v[0, 0 : loss_w.shape[0]]
+    loss_store.start()
+    grad_load.wait()
+    grad_store.start()
+    for c in range(pieces):
+        store(c).wait()
+    loss_store.wait()
+    grad_store.wait()
 
 
 def local(n, ngy, queries, positions, queue, new_keys, step):
@@ -254,6 +291,8 @@
         in_specs=[anywhere] * 4,
         out_specs=(vmem, vmem, anywhere),
         scratch_shapes=[
+            pltpu.VMEM((n * ngy, nk_dev, width), BF16),
+            dma((n,)),
             pltpu.VMEM((key_dev, width), BF16),
             pltpu.VMEM((n, q_dev, width), BF16),
             pltpu.VMEM((n, 1, LANES), jnp.int32),
@@ -269,7 +308,7 @@
             dma((n,)), dma((n,)), dma((n,)), dma((n,)),
         ],
         compiler_params=pltpu.CompilerParams(
-            collective_id=0, has_side_effects=True, vmem_limit_bytes=48 * 2**20
+            collective_id=0, has_side_effects=True, vmem_limit_bytes=62 * 2**20
         ),
         cost_estimate=pl.CostEstimate(
             flops=6 * rows * key_dev * width,
@@ -285,9 +324,19 @@
             jax.ShapeDtypeStruct((q_dev, width), BF16),
             jax.ShapeDtypeStruct((key_dev, width), BF16),
         ),
-        in_specs=[pl.BlockSpec(memory_space=pltpu.SMEM), vmem, vmem, anywhere, anywhere],
-        out_specs=(vmem, vmem, anywhere),
-        scratch_shapes=[dma((1,))],
+        in_specs=[pl.BlockSpec(memory_space=pltpu.SMEM)] + [anywhere] * 4,
+        out_specs=(anywhere,) * 3,
+        scratch_shapes=[
+            pltpu.VMEM((1, LANES), F32),
+            pltpu.VMEM((q_dev,), F32),
+            pltpu.VMEM((q_dev, width), BF16),
+            pltpu.VMEM((key_dev, width), BF16),
+            dma((8,)),
+            dma((8,)),
+            dma((2,)),
+            dma((2,)),
+        ],
+        compiler_params=pltpu.CompilerParams(vmem_limit_bytes=62 * 2**20),
         name="finish",
     )(step, loss_row, grad, queue, arrived.reshape(key_dev, width))
 

time: 61.4 us -> 25.6 us (0.42)
  Pallas kernels: 54.9 us -> 24.2 us
  local copies, waits for them, and re-layouts: 4.78 us -> 0 us
    pallas_call x1, Pallas kernels: 34.2 us -> 2.14 us  [local(): pl.pallas_call(functools.partial(finish, n), out_shape=(jax.ShapeDtypeStr...]
    unnamed x14 -> x0, local copies, waits for them, and re-layouts: 4.78 us -> none
    pallas_call x1, Pallas kernels: 20.7 us -> 22 us  [local(): pl.pallas_call(functools.partial(exchange, n, ngy, scale), out_shape=(jax...]
where the time goes in v2:
time: 25.6 us; the launch traced here: 25.5 us
  Pallas kernels  24.2 us (95%)
  between operations  1.29 us (5%)
    pallas_call x1, Pallas kernels, local(): pl.pallas_call(functools.partial(exchange, n, ngy, scale), out_shape=(jax...  22 us
    pallas_call x1, Pallas kernels, local(): pl.pallas_call(functools.partial(finish, n), out_shape=(jax.ShapeDtypeStr...  2.14 us

profile of v2, /device:TPU:0, one launch (start us, length us, event | category | flops | bytes accessed | tf_op | source)
XLA Modules:
  0.0 25.5 jit_solution(14713483304966695953)
XLA Ops:
  1.3 22.0 %exchange.1 = (f32[1,128]{1,0:T(1,128)}, bf16[32,256]{1,0:T(8,128)(2,1)}, bf16[32,64,256]{2,1,0:T(8,128)(2,1)}) custom-call(bf16[32,256]{1,0:T(8,128)(2,1)} %q_ref.1, s32[32]{0:T(128)} %pos_ref.1, bf16[2048,256]{1,0:T(8,128)(2,1)} %queue_ref.3, bf16[64,256]{1,0:T(8,128)(2,1)} %nk_ref.1), custom_call_target="tpu_custom_call" | custom-call | flops 805306368 | bytes 2097152 | tf_op jit(solution)/shard_map/exchange/pallas_call | solution.py:284
  23.3 2.1 %finish.1 = (f32[32]{0:T(128)}, bf16[32,256]{1,0:T(8,128)(2,1)}, bf16[2048,256]{1,0:T(8,128)(2,1)}) custom-call(s32[1]{0:T(128)S(6)} %copy.8.step_ref, f32[1,128]{1,0:T(1,128)} %get-tuple-element.6.loss_ref, bf16[32,256]{1,0:T(8,128)(2,1)} %get-tuple-element.7.grad_ref, bf16[2048,256]{1,0:T(8,128)(2,1)} %queue_ref.3, bf16[2048,256]{1,0:T(8,128)(2,1)} %bitcast.1), custom_call_target="tpu_custom_call" | custom-call | tf_op jit(solution)/shard_map/finish/pallas_call | solution.py:320

commit v3 on v2

--- a/solution.py
+++ b/solution.py
@@ -32,7 +32,7 @@
     q_ref, pos_ref, queue_ref, nk_ref,
     loss_ref, grad_ref, gathered_ref,
     arrived_ref, keep_sem, keys, q_all, p_all, pos_v, part_send, part_recv, stat_send, stat_recv,
-    local_sem, q_ss, q_rs, p_ss, p_rs, z_ss, z_rs, k_ss, f_ss, k_rs, g_ss, g_rs, s_ss, s_rs,
+    local_sem, q_ss, q_rs, p_ss, p_rs, z_ss, z_rs, k_ss, k_rs, r_ss, f_ss, f_rs, g_ss, g_rs, s_ss, s_rs,
 ):
     i = lax.axis_index("gx")
     j = lax.axis_index("gy")
@@ -83,52 +83,77 @@
 
     gx_peers(start_queries)
 
-    def z_copy(p):
-        return send(arrived_ref.at[i * ngy + j], arrived_ref.at[i * ngy + j], z_ss.at[p], z_rs.at[j], (i, p))
-
-    own_new.wait()
-    gy_peers(lambda p: z_copy(p).start())
+    square = n == 8
+    core = lax.rem(i, 2)
+    chip = i // 2
+    partner = i + 1 - 2 * core
+    low_bit, high_bit = lax.rem(chip, 2), chip // 2
+    side_a = (high_bit * 2 + 1 - low_bit) * 2 + core
+    side_b = ((1 - high_bit) * 2 + low_bit) * 2 + core
 
     def wait_in(dst, sem):
         pltpu.make_async_copy(dst, dst, sem).wait()
 
-    partner = i + 1 - 2 * lax.rem(i, 2)
+    def block(k, z):
+        return arrived_ref.at[k * ngy + z]
 
     def rows_of(k):
         return arrived_ref.at[pl.ds(k * ngy, ngy)]
 
+    def z_copy(p):
+        return send(block(i, j), block(i, j), z_ss.at[p], z_rs.at[j], (i, p))
+
+    def side_copy(z, side, to):
+        return send(block(i, z), block(i, z), k_ss.at[side * ngy + z], k_rs.at[i * ngy + z], (to, j))
+
+    def relay_copy(z):
+        k, to = (side_a, side_b) if z % 2 == 0 else (side_b, side_a)
+        return send(block(k, z), block(k, z), r_ss.at[z], k_rs.at[k * ngy + z], (to, j))
+
     def k_copy(p):
         return send(rows_of(i), rows_of(i), k_ss.at[p], k_rs.at[i], (p, j))
 
     def f_copy(k):
-        return send(rows_of(k), rows_of(k), f_ss.at[k], k_rs.at[k], (partner, j))
+        return send(rows_of(k), rows_of(k), f_ss.at[k], f_rs.at[k], (partner, j))
+
+    def keep(k):
+        return pltpu.make_async_copy(rows_of(k), gathered_ref.at[pl.ds(k * ngy, ngy)], keep_sem.at[k])
 
     def same_core(body):
         for d in range(2, n, 2):
             body(lax.rem(i + d, n))
 
-    load_keys.wait()
+    def to_sides(z):
+        side_copy(z, 0, side_a).start()
+        side_copy(z, 1, side_b).start()
+
+    own_new.wait()
+    gy_peers(lambda p: z_copy(p).start())
+    if square:
+        to_sides(j)
 
     def wait_queries(p):
         wait_in(p_all.at[p], p_rs.at[p])
         wait_in(q_all.at[p], q_rs.at[p])
 
     gx_peers(wait_queries)
-
-    gy_peers(lambda p: wait_in(arrived_ref.at[i * ngy + p], z_rs.at[p]))
-    same_core(lambda p: k_copy(p).start())
-    k_copy(partner).start()
-
-    def keep(k):
-        return pltpu.make_async_copy(rows_of(k), gathered_ref.at[pl.ds(k * ngy, ngy)], keep_sem.at[k])
-
+    load_keys.wait()
+
+    def next_block(z):
+        wait_in(block(i, z), z_rs.at[z])
+        if square:
+            to_sides(z)
+
+    gy_peers(next_block)
+    if not square:
+        same_core(lambda p: k_copy(p).start())
+    f_copy(i).start()
     keep(i).start()
 
-    group = min(n, 256 // q_dev)
+    group = n // 2 if square else min(n, 256 // q_dev)
     rows = group * q_dev
 
-    def work(c):
-        at = c * group
+    def work(at):
         columns = [to_column(p_all[at + b].astype(F32), diag) for b in range(group)]
         target = jnp.concatenate(columns, axis=0).astype(jnp.int32) - i * key_dev
         q = q_all[pl.ds(at, group)].reshape(rows, width)
@@ -136,12 +161,12 @@
         scores = lax.dot_general(q, slab, (((1,), (1,)), ((), ())), preferred_element_type=F32) * scale
         hits = lax.broadcasted_iota(jnp.int32, scores.shape, 1) == target
         top = jnp.max(scores, axis=1, keepdims=True)
-        positive = jnp.sum(jnp.where(hits, scores, 0.0), axis=1, keepdims=True)
         powers = jnp.exp(scores - top)
         total = jnp.sum(powers, axis=1, keepdims=True)
         others = jnp.where(hits, 0.0, powers).astype(BF16)
         part = jnp.dot(others, slab, preferred_element_type=F32)
         row = jnp.dot(hits.astype(F32).astype(BF16), slab, preferred_element_type=F32)
+        positive = jnp.sum(q.astype(F32) * row, axis=1, keepdims=True) * scale
         high = part.astype(BF16)
         low = part - high.astype(F32)
         inside = jnp.logical_and(target >= 0, target < key_dev)
@@ -155,11 +180,6 @@
             stat_send[at + b, 2:3] = to_row(positive[span], diag)
             stat_send[at + b, 3:4] = jnp.zeros((1, LANES), F32)
 
-    if n == group:
-        work(0)
-    else:
-        pl.loop(0, n // group)(work)
-
     def g_copy(p):
         return send(part_send.at[p], part_recv.at[i], g_ss.at[p], g_rs.at[i], (p, j))
 
@@ -170,16 +190,45 @@
         s_copy(p).start()
         g_copy(p).start()
 
-    gx_peers(start_parts)
+    if square:
+        far = (1 - high_bit) * group
+        work(far)
+        for b in range(group):
+            start_parts(far + b)
+        for z in range(ngy):
+            k = side_a if z % 2 == 0 else side_b
+            wait_in(block(k, z), k_rs.at[k * ngy + z])
+            relay_copy(z).start()
+        near = high_bit * group
+        work(near)
+        for d in range(1, group):
+            start_parts(near + lax.rem(i - near + d, group))
+    else:
+        pl.loop(0, n // group)(lambda c: work(c * group))
+        gx_peers(start_parts)
     part_recv[i] = part_send[i]
     stat_recv[i] = stat_send[i]
 
     def pass_on(k):
-        wait_in(rows_of(k), k_rs.at[k])
         f_copy(k).start()
         keep(k).start()
 
-    same_core(pass_on)
+    if square:
+        across = 6 - 2 * chip + core
+        for z in range(ngy):
+            k = side_b if z % 2 == 0 else side_a
+            wait_in(block(k, z), k_rs.at[k * ngy + z])
+        pass_on(side_a)
+        pass_on(side_b)
+        for z in range(ngy):
+            wait_in(block(across, z), k_rs.at[across * ngy + z])
+        pass_on(across)
+    else:
+        def receive(k):
+            wait_in(rows_of(k), k_rs.at[k])
+            pass_on(k)
+
+        same_core(receive)
 
     gx_peers(lambda p: wait_in(stat_recv.at[p], s_rs.at[p]))
     top = stat_recv[0, 0:1]
@@ -207,7 +256,7 @@
 
     for d in range(0, n, 2):
         k = lax.rem(partner + d, n)
-        wait_in(rows_of(k), k_rs.at[k])
+        wait_in(rows_of(k), f_rs.at[k])
         keep(k).start()
 
     def end_sends(p):
@@ -218,8 +267,14 @@
 
     gx_peers(end_sends)
     gy_peers(lambda p: z_copy(p).wait_send())
-    same_core(lambda p: k_copy(p).wait_send())
-    k_copy(partner).wait_send()
+    if square:
+        for z in range(ngy):
+            side_copy(z, 0, side_a).wait_send()
+            side_copy(z, 1, side_b).wait_send()
+            relay_copy(z).wait_send()
+    else:
+        same_core(lambda p: k_copy(p).wait_send())
+    f_copy(i).wait_send()
     same_core(lambda k: f_copy(k).wait_send())
     for k in range(n):
         keep(k).wait()
@@ -304,7 +359,7 @@
             dma((4,)),
             dma((n,)), dma((n,)), dma((n,)), dma((n,)),
             dma((ngy,)), dma((ngy,)),
-            dma((n,)), dma((n,)), dma((n,)),
+            dma((max(n, 2 * ngy),)), dma((n * ngy,)), dma((ngy,)), dma((n,)), dma((n,)),
             dma((n,)), dma((n,)), dma((n,)), dma((n,)),
         ],
         compiler_params=pltpu.CompilerParams(

time: 25.6 us -> 24.9 us (0.973)
  Pallas kernels: 24.2 us -> 23.4 us
    pallas_call x1, Pallas kernels: 22 us -> 21.3 us  [local(): pl.pallas_call(functools.partial(exchange, n, ngy, scale), out_shape=(jax...]
where the time goes in v3:
time: 24.9 us; the launch traced here: 24.7 us
  Pallas kernels  23.4 us (94%)
  between operations  1.29 us (5%)
    pallas_call x1, Pallas kernels, local(): pl.pallas_call(functools.partial(exchange, n, ngy, scale), out_shape=(jax...  21.3 us
    pallas_call x1, Pallas kernels, local(): pl.pallas_call(functools.partial(finish, n), out_shape=(jax.ShapeDtypeStr...  2.14 us

profile of v3, /device:TPU:0, one launch (start us, length us, event | category | flops | bytes accessed | tf_op | source)
XLA Modules:
  0.0 24.7 jit_solution(2358692918356844981)
XLA Ops:
  1.3 21.3 %exchange.1 = (f32[1,128]{1,0:T(1,128)}, bf16[32,256]{1,0:T(8,128)(2,1)}, bf16[32,64,256]{2,1,0:T(8,128)(2,1)}) custom-call(bf16[32,256]{1,0:T(8,128)(2,1)} %q_ref.1, s32[32]{0:T(128)} %pos_ref.1, bf16[2048,256]{1,0:T(8,128)(2,1)} %queue_ref.3, bf16[64,256]{1,0:T(8,128)(2,1)} %nk_ref.1), custom_call_target="tpu_custom_call" | custom-call | flops 805306368 | bytes 2097152 | tf_op jit(solution)/shard_map/exchange/pallas_call | solution.py:339
  22.5 2.1 %finish.1 = (f32[32]{0:T(128)}, bf16[32,256]{1,0:T(8,128)(2,1)}, bf16[2048,256]{1,0:T(8,128)(2,1)}) custom-call(s32[1]{0:T(128)S(6)} %copy.8.step_ref, f32[1,128]{1,0:T(1,128)} %get-tuple-element.6.loss_ref, bf16[32,256]{1,0:T(8,128)(2,1)} %get-tuple-element.7.grad_ref, bf16[2048,256]{1,0:T(8,128)(2,1)} %queue_ref.3, bf16[2048,256]{1,0:T(8,128)(2,1)} %bitcast.1), custom_call_target="tpu_custom_call" | custom-call | tf_op jit(solution)/shard_map/finish/pallas_call | solution.py:375

commit v4 on v3

--- a/solution.py
+++ b/solution.py
@@ -31,7 +31,7 @@
     n, ngy, scale,
     q_ref, pos_ref, queue_ref, nk_ref,
     loss_ref, grad_ref, gathered_ref,
-    arrived_ref, keep_sem, keys, q_all, p_all, pos_v, part_send, part_recv, stat_send, stat_recv,
+    arrived_ref, keep_sem, keys_t, keys, q_all, p_all, pos_v, part_send, part_recv, stat_send, stat_recv,
     local_sem, q_ss, q_rs, p_ss, p_rs, z_ss, z_rs, k_ss, k_rs, r_ss, f_ss, f_rs, g_ss, g_rs, s_ss, s_rs,
 ):
     i = lax.axis_index("gx")
@@ -113,11 +113,14 @@
     def k_copy(p):
         return send(rows_of(i), rows_of(i), k_ss.at[p], k_rs.at[i], (p, j))
 
+    def kept(k):
+        return gathered_ref.at[pl.ds(k * ngy, ngy)]
+
     def f_copy(k):
-        return send(rows_of(k), rows_of(k), f_ss.at[k], f_rs.at[k], (partner, j))
+        return send(rows_of(k), kept(k), f_ss.at[k], f_rs.at[k], (partner, j))
 
     def keep(k):
-        return pltpu.make_async_copy(rows_of(k), gathered_ref.at[pl.ds(k * ngy, ngy)], keep_sem.at[k])
+        return pltpu.make_async_copy(rows_of(k), kept(k), keep_sem.at[k])
 
     def same_core(body):
         for d in range(2, n, 2):
@@ -136,19 +139,20 @@
         wait_in(p_all.at[p], p_rs.at[p])
         wait_in(q_all.at[p], q_rs.at[p])
 
-    gx_peers(wait_queries)
-    load_keys.wait()
+    def spread():
+        gy_peers(next_block)
+        if not square:
+            same_core(lambda p: k_copy(p).start())
+        f_copy(i).start()
+        keep(i).start()
 
     def next_block(z):
         wait_in(block(i, z), z_rs.at[z])
         if square:
             to_sides(z)
 
-    gy_peers(next_block)
-    if not square:
-        same_core(lambda p: k_copy(p).start())
-    f_copy(i).start()
-    keep(i).start()
+    load_keys.wait()
+    keys_t[...] = keys[...].T
 
     group = n // 2 if square else min(n, 256 // q_dev)
     rows = group * q_dev
@@ -158,7 +162,7 @@
         target = jnp.concatenate(columns, axis=0).astype(jnp.int32) - i * key_dev
         q = q_all[pl.ds(at, group)].reshape(rows, width)
         slab = keys[...]
-        scores = lax.dot_general(q, slab, (((1,), (1,)), ((), ())), preferred_element_type=F32) * scale
+        scores = jnp.dot(q, keys_t[...], preferred_element_type=F32) * scale
         hits = lax.broadcasted_iota(jnp.int32, scores.shape, 1) == target
         top = jnp.max(scores, axis=1, keepdims=True)
         powers = jnp.exp(scores - top)
@@ -192,18 +196,26 @@
 
     if square:
         far = (1 - high_bit) * group
+        for b in range(group):
+            wait_queries(far + b)
         work(far)
         for b in range(group):
             start_parts(far + b)
+        spread()
+        near = high_bit * group
+        others = [near + lax.rem(i - near + d, group) for d in range(1, group)]
+        for p in others:
+            wait_queries(p)
+        work(near)
+        for p in others:
+            start_parts(p)
         for z in range(ngy):
             k = side_a if z % 2 == 0 else side_b
             wait_in(block(k, z), k_rs.at[k * ngy + z])
             relay_copy(z).start()
-        near = high_bit * group
-        work(near)
-        for d in range(1, group):
-            start_parts(near + lax.rem(i - near + d, group))
     else:
+        gx_peers(wait_queries)
+        spread()
         pl.loop(0, n // group)(lambda c: work(c * group))
         gx_peers(start_parts)
     part_recv[i] = part_send[i]
@@ -256,8 +268,7 @@
 
     for d in range(0, n, 2):
         k = lax.rem(partner + d, n)
-        wait_in(rows_of(k), f_rs.at[k])
-        keep(k).start()
+        wait_in(kept(k), f_rs.at[k])
 
     def end_sends(p):
         p_copy(p).wait_send()
@@ -276,8 +287,8 @@
         same_core(lambda p: k_copy(p).wait_send())
     f_copy(i).wait_send()
     same_core(lambda k: f_copy(k).wait_send())
-    for k in range(n):
-        keep(k).wait()
+    keep(i).wait()
+    same_core(lambda k: keep(k).wait())
 
 
 def finish(
@@ -348,6 +359,7 @@
         scratch_shapes=[
             pltpu.VMEM((n * ngy, nk_dev, width), BF16),
             dma((n,)),
+            pltpu.VMEM((width, key_dev), BF16),
             pltpu.VMEM((key_dev, width), BF16),
             pltpu.VMEM((n, q_dev, width), BF16),
             pltpu.VMEM((n, 1, LANES), jnp.int32),

time: 24.9 us -> 26.8 us (1.076)
  Pallas kernels: 23.4 us -> 25.4 us
    pallas_call x1, Pallas kernels: 21.3 us -> 23.2 us  [local(): pl.pallas_call(functools.partial(exchange, n, ngy, scale), out_shape=(jax...]
where the time goes in v4:
time: 26.8 us; the launch traced here: 26.7 us
  Pallas kernels  25.4 us (95%)
  between operations  1.29 us (5%)
    pallas_call x1, Pallas kernels, local(): pl.pallas_call(functools.partial(exchange, n, ngy, scale), out_shape=(jax...  23.2 us
    pallas_call x1, Pallas kernels, local(): pl.pallas_call(functools.partial(finish, n), out_shape=(jax.ShapeDtypeStr...  2.14 us

profile of v4, /device:TPU:0, one launch (start us, length us, event | category | flops | bytes accessed | tf_op | source)
XLA Modules:
  0.0 26.7 jit_solution(2942904557711741030)
XLA Ops:
  1.3 23.2 %exchange.1 = (f32[1,128]{1,0:T(1,128)}, bf16[32,256]{1,0:T(8,128)(2,1)}, bf16[32,64,256]{2,1,0:T(8,128)(2,1)}) custom-call(bf16[32,256]{1,0:T(8,128)(2,1)} %q_ref.1, s32[32]{0:T(128)} %pos_ref.1, bf16[2048,256]{1,0:T(8,128)(2,1)} %queue_ref.3, bf16[64,256]{1,0:T(8,128)(2,1)} %nk_ref.1), custom_call_target="tpu_custom_call" | custom-call | flops 805306368 | bytes 2097152 | tf_op jit(solution)/shard_map/exchange/pallas_call | solution.py:350
  24.5 2.1 %finish.1 = (f32[32]{0:T(128)}, bf16[32,256]{1,0:T(8,128)(2,1)}, bf16[2048,256]{1,0:T(8,128)(2,1)}) custom-call(s32[1]{0:T(128)S(6)} %copy.8.step_ref, f32[1,128]{1,0:T(1,128)} %get-tuple-element.6.loss_ref, bf16[32,256]{1,0:T(8,128)(2,1)} %get-tuple-element.7.grad_ref, bf16[2048,256]{1,0:T(8,128)(2,1)} %queue_ref.3, bf16[2048,256]{1,0:T(8,128)(2,1)} %bitcast.1), custom_call_target="tpu_custom_call" | custom-call | tf_op jit(solution)/shard_map/finish/pallas_call | solution.py:387

commit v5 on v2

--- a/solution.py
+++ b/solution.py
@@ -32,7 +32,7 @@
     q_ref, pos_ref, queue_ref, nk_ref,
     loss_ref, grad_ref, gathered_ref,
     arrived_ref, keep_sem, keys, q_all, p_all, pos_v, part_send, part_recv, stat_send, stat_recv,
-    local_sem, q_ss, q_rs, p_ss, p_rs, z_ss, z_rs, k_ss, f_ss, k_rs, g_ss, g_rs, s_ss, s_rs,
+    local_sem, q_ss, q_rs, p_ss, p_rs, z_ss, z_rs, k_ss, k_rs, f_ss, f_rs, g_ss, g_rs, s_ss, s_rs,
 ):
     i = lax.axis_index("gx")
     j = lax.axis_index("gy")
@@ -83,52 +83,70 @@
 
     gx_peers(start_queries)
 
-    def z_copy(p):
-        return send(arrived_ref.at[i * ngy + j], arrived_ref.at[i * ngy + j], z_ss.at[p], z_rs.at[j], (i, p))
-
-    own_new.wait()
-    gy_peers(lambda p: z_copy(p).start())
+    by_block = n * ngy <= 32
+    core = lax.rem(i, 2)
+    partner = i + 1 - 2 * core
 
     def wait_in(dst, sem):
         pltpu.make_async_copy(dst, dst, sem).wait()
 
-    partner = i + 1 - 2 * lax.rem(i, 2)
+    def block(k, z):
+        return arrived_ref.at[k * ngy + z]
 
     def rows_of(k):
         return arrived_ref.at[pl.ds(k * ngy, ngy)]
 
+    def z_copy(p):
+        return send(block(i, j), block(i, j), z_ss.at[p], z_rs.at[j], (i, p))
+
+    def b_copy(p, z):
+        return send(block(i, z), block(i, z), k_ss.at[p * ngy + z], k_rs.at[i * ngy + z], (p, j))
+
     def k_copy(p):
         return send(rows_of(i), rows_of(i), k_ss.at[p], k_rs.at[i], (p, j))
 
+    def kept(k):
+        return gathered_ref.at[pl.ds(k * ngy, ngy)]
+
     def f_copy(k):
-        return send(rows_of(k), rows_of(k), f_ss.at[k], k_rs.at[k], (partner, j))
+        return send(rows_of(k), kept(k), f_ss.at[k], f_rs.at[k], (partner, j))
+
+    def keep(k):
+        return pltpu.make_async_copy(rows_of(k), kept(k), keep_sem.at[k])
 
     def same_core(body):
         for d in range(2, n, 2):
             body(lax.rem(i + d, n))
 
-    load_keys.wait()
+    def go_on(z):
+        same_core(lambda p: b_copy(p, z).start())
+
+    own_new.wait()
+    gy_peers(lambda p: z_copy(p).start())
+    if by_block:
+        go_on(j)
 
     def wait_queries(p):
         wait_in(p_all.at[p], p_rs.at[p])
         wait_in(q_all.at[p], q_rs.at[p])
 
+    def next_block(z):
+        wait_in(block(i, z), z_rs.at[z])
+        if by_block:
+            go_on(z)
+
+    gy_peers(next_block)
+    if not by_block:
+        same_core(lambda p: k_copy(p).start())
+    f_copy(i).start()
+    keep(i).start()
     gx_peers(wait_queries)
-
-    gy_peers(lambda p: wait_in(arrived_ref.at[i * ngy + p], z_rs.at[p]))
-    same_core(lambda p: k_copy(p).start())
-    k_copy(partner).start()
-
-    def keep(k):
-        return pltpu.make_async_copy(rows_of(k), gathered_ref.at[pl.ds(k * ngy, ngy)], keep_sem.at[k])
-
-    keep(i).start()
+    load_keys.wait()
 
     group = min(n, 256 // q_dev)
     rows = group * q_dev
 
-    def work(c):
-        at = c * group
+    def work(at):
         columns = [to_column(p_all[at + b].astype(F32), diag) for b in range(group)]
         target = jnp.concatenate(columns, axis=0).astype(jnp.int32) - i * key_dev
         q = q_all[pl.ds(at, group)].reshape(rows, width)
@@ -136,12 +154,12 @@
         scores = lax.dot_general(q, slab, (((1,), (1,)), ((), ())), preferred_element_type=F32) * scale
         hits = lax.broadcasted_iota(jnp.int32, scores.shape, 1) == target
         top = jnp.max(scores, axis=1, keepdims=True)
-        positive = jnp.sum(jnp.where(hits, scores, 0.0), axis=1, keepdims=True)
         powers = jnp.exp(scores - top)
         total = jnp.sum(powers, axis=1, keepdims=True)
         others = jnp.where(hits, 0.0, powers).astype(BF16)
         part = jnp.dot(others, slab, preferred_element_type=F32)
         row = jnp.dot(hits.astype(F32).astype(BF16), slab, preferred_element_type=F32)
+        positive = jnp.sum(q.astype(F32) * row, axis=1, keepdims=True) * scale
         high = part.astype(BF16)
         low = part - high.astype(F32)
         inside = jnp.logical_and(target >= 0, target < key_dev)
@@ -155,27 +173,30 @@
             stat_send[at + b, 2:3] = to_row(positive[span], diag)
             stat_send[at + b, 3:4] = jnp.zeros((1, LANES), F32)
 
+    def g_copy(p):
+        return send(part_send.at[p], part_recv.at[i], g_ss.at[p], g_rs.at[i], (p, j))
+
+    def s_copy(p):
+        return send(stat_send.at[p], stat_recv.at[i], s_ss.at[p], s_rs.at[i], (p, j))
+
+    def start_parts(p):
+        s_copy(p).start()
+        g_copy(p).start()
+
     if n == group:
         work(0)
     else:
-        pl.loop(0, n // group)(work)
-
-    def g_copy(p):
-        return send(part_send.at[p], part_recv.at[i], g_ss.at[p], g_rs.at[i], (p, j))
-
-    def s_copy(p):
-        return send(stat_send.at[p], stat_recv.at[i], s_ss.at[p], s_rs.at[i], (p, j))
-
-    def start_parts(p):
-        s_copy(p).start()
-        g_copy(p).start()
-
+        pl.loop(0, n // group)(lambda c: work(c * group))
     gx_peers(start_parts)
     part_recv[i] = part_send[i]
     stat_recv[i] = stat_send[i]
 
     def pass_on(k):
-        wait_in(rows_of(k), k_rs.at[k])
+        if by_block:
+            for z in range(ngy):
+                wait_in(block(k, z), k_rs.at[k * ngy + z])
+        else:
+            wait_in(rows_of(k), k_rs.at[k])
         f_copy(k).start()
         keep(k).start()
 
@@ -207,8 +228,7 @@
 
     for d in range(0, n, 2):
         k = lax.rem(partner + d, n)
-        wait_in(rows_of(k), k_rs.at[k])
-        keep(k).start()
+        wait_in(kept(k), f_rs.at[k])
 
     def end_sends(p):
         p_copy(p).wait_send()
@@ -218,11 +238,15 @@
 
     gx_peers(end_sends)
     gy_peers(lambda p: z_copy(p).wait_send())
-    same_core(lambda p: k_copy(p).wait_send())
-    k_copy(partner).wait_send()
+    if by_block:
+        for z in range(ngy):
+            same_core(lambda p: b_copy(p, z).wait_send())
+    else:
+        same_core(lambda p: k_copy(p).wait_send())
+    f_copy(i).wait_send()
     same_core(lambda k: f_copy(k).wait_send())
-    for k in range(n):
-        keep(k).wait()
+    keep(i).wait()
+    same_core(lambda k: keep(k).wait())
 
 
 def finish(
@@ -304,7 +328,7 @@
             dma((4,)),
             dma((n,)), dma((n,)), dma((n,)), dma((n,)),
             dma((ngy,)), dma((ngy,)),
-            dma((n,)), dma((n,)), dma((n,)),
+            dma((n * ngy,)), dma((n * ngy,)), dma((n,)), dma((n,)),
             dma((n,)), dma((n,)), dma((n,)), dma((n,)),
         ],
         compiler_params=pltpu.CompilerParams(

time: 25.6 us -> 22.8 us (0.89)
  Pallas kernels: 24.2 us -> 21.4 us
    pallas_call x1, Pallas kernels: 22 us -> 19.2 us  [local(): pl.pallas_call(functools.partial(exchange, n, ngy, scale), out_shape=(jax...]
where the time goes in v5:
time: 22.8 us; the launch traced here: 22.6 us
  Pallas kernels  21.4 us (94%)
  between operations  1.29 us (6%)
    pallas_call x1, Pallas kernels, local(): pl.pallas_call(functools.partial(exchange, n, ngy, scale), out_shape=(jax...  19.2 us
    pallas_call x1, Pallas kernels, local(): pl.pallas_call(functools.partial(finish, n), out_shape=(jax.ShapeDtypeStr...  2.14 us

profile of v5, /device:TPU:0, one launch (start us, length us, event | category | flops | bytes accessed | tf_op | source)
XLA Modules:
  0.0 22.6 jit_solution(12327694404348107125)
XLA Ops:
  1.3 19.2 %exchange.1 = (f32[1,128]{1,0:T(1,128)}, bf16[32,256]{1,0:T(8,128)(2,1)}, bf16[32,64,256]{2,1,0:T(8,128)(2,1)}) custom-call(bf16[32,256]{1,0:T(8,128)(2,1)} %q_ref.1, s32[32]{0:T(128)} %pos_ref.1, bf16[2048,256]{1,0:T(8,128)(2,1)} %queue_ref.3, bf16[64,256]{1,0:T(8,128)(2,1)} %nk_ref.1), custom_call_target="tpu_custom_call" | custom-call | flops 805306368 | bytes 2097152 | tf_op jit(solution)/shard_map/exchange/pallas_call | solution.py:308
  20.5 2.1 %finish.1 = (f32[32]{0:T(128)}, bf16[32,256]{1,0:T(8,128)(2,1)}, bf16[2048,256]{1,0:T(8,128)(2,1)}) custom-call(s32[1]{0:T(128)S(6)} %copy.8.step_ref, f32[1,128]{1,0:T(1,128)} %get-tuple-element.6.loss_ref, bf16[32,256]{1,0:T(8,128)(2,1)} %get-tuple-element.7.grad_ref, bf16[2048,256]{1,0:T(8,128)(2,1)} %queue_ref.3, bf16[2048,256]{1,0:T(8,128)(2,1)} %bitcast.1), custom_call_target="tpu_custom_call" | custom-call | tf_op jit(solution)/shard_map/finish/pallas_call | solution.py:344

commit v6 on v5

--- a/solution.py
+++ b/solution.py
@@ -77,12 +77,6 @@
     def p_copy(p):
         return send(p_all.at[i], p_all.at[i], p_ss.at[p], p_rs.at[i], (p, j))
 
-    def start_queries(p):
-        p_copy(p).start()
-        q_copy(p).start()
-
-    gx_peers(start_queries)
-
     by_block = n * ngy <= 32
     core = lax.rem(i, 2)
     partner = i + 1 - 2 * core
@@ -121,57 +115,41 @@
     def go_on(z):
         same_core(lambda p: b_copy(p, z).start())
 
-    own_new.wait()
-    gy_peers(lambda p: z_copy(p).start())
-    if by_block:
-        go_on(j)
-
-    def wait_queries(p):
-        wait_in(p_all.at[p], p_rs.at[p])
-        wait_in(q_all.at[p], q_rs.at[p])
-
-    def next_block(z):
-        wait_in(block(i, z), z_rs.at[z])
-        if by_block:
-            go_on(z)
-
-    gy_peers(next_block)
-    if not by_block:
-        same_core(lambda p: k_copy(p).start())
-    f_copy(i).start()
-    keep(i).start()
-    gx_peers(wait_queries)
-    load_keys.wait()
-
     group = min(n, 256 // q_dev)
     rows = group * q_dev
 
-    def work(at):
+    def find(at):
         columns = [to_column(p_all[at + b].astype(F32), diag) for b in range(group)]
         target = jnp.concatenate(columns, axis=0).astype(jnp.int32) - i * key_dev
+        hits = lax.broadcasted_iota(jnp.int32, (rows, key_dev), 1) == target
+        row = jnp.dot(hits.astype(F32).astype(BF16), keys[...], preferred_element_type=F32)
+        return target, row
+
+    def work(at, found, start_stats):
+        target, row = found
         q = q_all[pl.ds(at, group)].reshape(rows, width)
         slab = keys[...]
-        scores = lax.dot_general(q, slab, (((1,), (1,)), ((), ())), preferred_element_type=F32) * scale
-        hits = lax.broadcasted_iota(jnp.int32, scores.shape, 1) == target
-        top = jnp.max(scores, axis=1, keepdims=True)
-        powers = jnp.exp(scores - top)
+        raw = lax.dot_general(q, slab, (((1,), (1,)), ((), ())), preferred_element_type=F32)
+        hits = lax.broadcasted_iota(jnp.int32, raw.shape, 1) == target
+        top = jnp.max(raw, axis=1, keepdims=True)
+        powers = jnp.exp2((raw - top) * (scale * math.log2(math.e)))
         total = jnp.sum(powers, axis=1, keepdims=True)
         others = jnp.where(hits, 0.0, powers).astype(BF16)
+        positive = jnp.sum(jnp.where(hits, raw, 0.0), axis=1, keepdims=True)
+        for b in range(group):
+            span = slice(b * q_dev, (b + 1) * q_dev)
+            stat_send[at + b, 0:1] = to_row(top[span], diag) * scale
+            stat_send[at + b, 1:2] = to_row(total[span], diag)
+            stat_send[at + b, 2:3] = to_row(positive[span], diag) * scale
+            stat_send[at + b, 3:4] = jnp.zeros((1, LANES), F32)
+        start_stats()
         part = jnp.dot(others, slab, preferred_element_type=F32)
-        row = jnp.dot(hits.astype(F32).astype(BF16), slab, preferred_element_type=F32)
-        positive = jnp.sum(q.astype(F32) * row, axis=1, keepdims=True) * scale
         high = part.astype(BF16)
         low = part - high.astype(F32)
         inside = jnp.logical_and(target >= 0, target < key_dev)
         second = jnp.where(inside, row, low).astype(BF16)
         part_send[pl.ds(at, group), 0] = high.reshape(group, q_dev, width)
         part_send[pl.ds(at, group), 1] = second.reshape(group, q_dev, width)
-        for b in range(group):
-            span = slice(b * q_dev, (b + 1) * q_dev)
-            stat_send[at + b, 0:1] = to_row(top[span], diag)
-            stat_send[at + b, 1:2] = to_row(total[span], diag)
-            stat_send[at + b, 2:3] = to_row(positive[span], diag)
-            stat_send[at + b, 3:4] = jnp.zeros((1, LANES), F32)
 
     def g_copy(p):
         return send(part_send.at[p], part_recv.at[i], g_ss.at[p], g_rs.at[i], (p, j))
@@ -179,15 +157,34 @@
     def s_copy(p):
         return send(stat_send.at[p], stat_recv.at[i], s_ss.at[p], s_rs.at[i], (p, j))
 
-    def start_parts(p):
-        s_copy(p).start()
-        g_copy(p).start()
-
-    if n == group:
-        work(0)
+    def next_block(z):
+        wait_in(block(i, z), z_rs.at[z])
+        if by_block:
+            go_on(z)
+
+    own_new.wait()
+    gy_peers(lambda p: z_copy(p).start())
+    gx_peers(lambda p: p_copy(p).start())
+    gx_peers(lambda p: q_copy(p).start())
+    if by_block:
+        go_on(j)
+    load_keys.wait()
+    gx_peers(lambda p: wait_in(p_all.at[p], p_rs.at[p]))
+    whole = n == group
+    if whole:
+        found = find(0)
+    gy_peers(next_block)
+    if not by_block:
+        same_core(lambda p: k_copy(p).start())
+    f_copy(i).start()
+    keep(i).start()
+    gx_peers(lambda p: wait_in(q_all.at[p], q_rs.at[p]))
+    if whole:
+        work(0, found, lambda: gx_peers(lambda p: s_copy(p).start()))
     else:
-        pl.loop(0, n // group)(lambda c: work(c * group))
-    gx_peers(start_parts)
+        pl.loop(0, n // group)(lambda c: work(c * group, find(c * group), lambda: None))
+        gx_peers(lambda p: s_copy(p).start())
+    gx_peers(lambda p: g_copy(p).start())
     part_recv[i] = part_send[i]
     stat_recv[i] = stat_send[i]
 

time: 22.8 us -> 24.1 us (1.057)
  Pallas kernels: 21.4 us -> 22.6 us
    pallas_call x1, Pallas kernels: 19.2 us -> 20.5 us  [local(): pl.pallas_call(functools.partial(exchange, n, ngy, scale), out_shape=(jax...]
where the time goes in v6:
time: 24.1 us; the launch traced here: 23.9 us
  Pallas kernels  22.6 us (94%)
  between operations  1.29 us (5%)
    pallas_call x1, Pallas kernels, local(): pl.pallas_call(functools.partial(exchange, n, ngy, scale), out_shape=(jax...  20.5 us
    pallas_call x1, Pallas kernels, local(): pl.pallas_call(functools.partial(finish, n), out_shape=(jax.ShapeDtypeStr...  2.14 us

profile of v6, /device:TPU:0, one launch (start us, length us, event | category | flops | bytes accessed | tf_op | source)
XLA Modules:
  0.0 23.9 jit_solution(3342139018997402119)
XLA Ops:
  1.3 20.5 %exchange.1 = (f32[1,128]{1,0:T(1,128)}, bf16[32,256]{1,0:T(8,128)(2,1)}, bf16[32,64,256]{2,1,0:T(8,128)(2,1)}) custom-call(bf16[32,256]{1,0:T(8,128)(2,1)} %q_ref.1, s32[32]{0:T(128)} %pos_ref.1, bf16[2048,256]{1,0:T(8,128)(2,1)} %queue_ref.3, bf16[64,256]{1,0:T(8,128)(2,1)} %nk_ref.1), custom_call_target="tpu_custom_call" | custom-call | flops 805306368 | bytes 2097152 | tf_op jit(solution)/shard_map/exchange/pallas_call | solution.py:305
  21.7 2.1 %finish.1 = (f32[32]{0:T(128)}, bf16[32,256]{1,0:T(8,128)(2,1)}, bf16[2048,256]{1,0:T(8,128)(2,1)}) custom-call(s32[1]{0:T(128)S(6)} %copy.8.step_ref, f32[1,128]{1,0:T(1,128)} %get-tuple-element.6.loss_ref, bf16[32,256]{1,0:T(8,128)(2,1)} %get-tuple-element.7.grad_ref, bf16[2048,256]{1,0:T(8,128)(2,1)} %queue_ref.3, bf16[2048,256]{1,0:T(8,128)(2,1)} %bitcast.1), custom_call_target="tpu_custom_call" | custom-call | tf_op jit(solution)/shard_map/finish/pallas_call | solution.py:341

commit v7 on v6

--- a/solution.py
+++ b/solution.py
@@ -30,8 +30,8 @@
 def exchange(
     n, ngy, scale,
     q_ref, pos_ref, queue_ref, nk_ref,
-    loss_ref, grad_ref, gathered_ref,
-    arrived_ref, keep_sem, keys, q_all, p_all, pos_v, part_send, part_recv, stat_send, stat_recv,
+    loss_out, grad_out, gathered_ref,
+    loss_ref, grad_ref, result_sem, arrived_ref, keep_sem, keys, q_all, p_all, pos_v, part_send, part_recv, stat_send, stat_recv,
     local_sem, q_ss, q_rs, p_ss, p_rs, z_ss, z_rs, k_ss, k_rs, f_ss, f_rs, g_ss, g_rs, s_ss, s_rs,
 ):
     i = lax.axis_index("gx")
@@ -49,8 +49,9 @@
             body(lax.rem(i + d, n))
 
     def gy_peers(body):
+        turn = 1 - 2 * ((2 * j) // ngy)
         for d in range(1, ngy):
-            body(lax.rem(j + d, ngy))
+            body(lax.rem(j + turn * d + ngy, ngy))
 
     load_pos = pltpu.make_async_copy(pos_ref, pos_v, local_sem.at[0])
     load_q = pltpu.make_async_copy(q_ref, q_all.at[i], local_sem.at[1])
@@ -168,16 +169,16 @@
     gx_peers(lambda p: q_copy(p).start())
     if by_block:
         go_on(j)
+    gy_peers(next_block)
+    if not by_block:
+        same_core(lambda p: k_copy(p).start())
+    f_copy(i).start()
+    keep(i).start()
     load_keys.wait()
     gx_peers(lambda p: wait_in(p_all.at[p], p_rs.at[p]))
     whole = n == group
     if whole:
         found = find(0)
-    gy_peers(next_block)
-    if not by_block:
-        same_core(lambda p: k_copy(p).start())
-    f_copy(i).start()
-    keep(i).start()
     gx_peers(lambda p: wait_in(q_all.at[p], q_rs.at[p]))
     if whole:
         work(0, found, lambda: gx_peers(lambda p: s_copy(p).start()))
@@ -223,9 +224,10 @@
         grad = grad + factors[s] * first + jnp.where(inside, at_positive, factors[s]) * second
     grad_ref[...] = (grad * scale).astype(BF16)
 
-    for d in range(0, n, 2):
-        k = lax.rem(partner + d, n)
-        wait_in(kept(k), f_rs.at[k])
+    loss_store = pltpu.make_async_copy(loss_ref, loss_out, result_sem.at[0])
+    grad_store = pltpu.make_async_copy(grad_ref, grad_out, result_sem.at[1])
+    loss_store.start()
+    grad_store.start()
 
     def end_sends(p):
         p_copy(p).wait_send()
@@ -241,9 +243,14 @@
     else:
         same_core(lambda p: k_copy(p).wait_send())
     f_copy(i).wait_send()
+    keep(i).wait()
     same_core(lambda k: f_copy(k).wait_send())
-    keep(i).wait()
     same_core(lambda k: keep(k).wait())
+    for d in range(0, n, 2):
+        k = lax.rem(partner + d, n)
+        wait_in(kept(k), f_rs.at[k])
+    loss_store.wait()
+    grad_store.wait()
 
 
 def finish(
@@ -299,7 +306,6 @@
     nk_dev = new_keys.shape[0]
     scale = 2.0 / math.sqrt(width)
     anywhere = pl.BlockSpec(memory_space=pl.ANY)
-    vmem = pl.BlockSpec(memory_space=pltpu.VMEM)
     dma = pltpu.SemaphoreType.DMA
     rows = n * q_dev
     loss_row, grad, arrived = pl.pallas_call(
@@ -310,8 +316,11 @@
             jax.ShapeDtypeStruct((n * ngy, nk_dev, width), BF16),
         ),
         in_specs=[anywhere] * 4,
-        out_specs=(vmem, vmem, anywhere),
+        out_specs=(anywhere,) * 3,
         scratch_shapes=[
+            pltpu.VMEM((1, LANES), F32),
+            pltpu.VMEM((q_dev, width), BF16),
+            dma((2,)),
             pltpu.VMEM((n * ngy, nk_dev, width), BF16),
             dma((n,)),
             pltpu.VMEM((key_dev, width), BF16),

time: 24.1 us -> 22.7 us (0.942)
  Pallas kernels: 22.6 us -> 21.3 us
    pallas_call x1, Pallas kernels: 20.5 us -> 19.2 us  [local(): pl.pallas_call(functools.partial(exchange, n, ngy, scale), out_shape=(jax...]
where the time goes in v7:
time: 22.7 us; the launch traced here: 22.6 us
  Pallas kernels  21.3 us (94%)
  between operations  1.29 us (6%)
    pallas_call x1, Pallas kernels, local(): pl.pallas_call(functools.partial(exchange, n, ngy, scale), out_shape=(jax...  19.2 us
    pallas_call x1, Pallas kernels, local(): pl.pallas_call(functools.partial(finish, n), out_shape=(jax.ShapeDtypeStr...  2.14 us

profile of v7, /device:TPU:0, one launch (start us, length us, event | category | flops | bytes accessed | tf_op | source)
XLA Modules:
  0.0 22.6 jit_solution(5925954337344730299)
XLA Ops:
  1.3 19.2 %exchange.1 = (f32[1,128]{1,0:T(1,128)}, bf16[32,256]{1,0:T(8,128)(2,1)}, bf16[32,64,256]{2,1,0:T(8,128)(2,1)}) custom-call(bf16[32,256]{1,0:T(8,128)(2,1)} %q_ref.1, s32[32]{0:T(128)} %pos_ref.1, bf16[2048,256]{1,0:T(8,128)(2,1)} %queue_ref.3, bf16[64,256]{1,0:T(8,128)(2,1)} %nk_ref.1), custom_call_target="tpu_custom_call" | custom-call | flops 805306368 | bytes 2097152 | tf_op jit(solution)/shard_map/exchange/pallas_call | solution.py:311
  20.4 2.1 %finish.1 = (f32[32]{0:T(128)}, bf16[32,256]{1,0:T(8,128)(2,1)}, bf16[2048,256]{1,0:T(8,128)(2,1)}) custom-call(s32[1]{0:T(128)S(6)} %copy.8.step_ref, f32[1,128]{1,0:T(1,128)} %get-tuple-element.6.loss_ref, bf16[32,256]{1,0:T(8,128)(2,1)} %get-tuple-element.7.grad_ref, bf16[2048,256]{1,0:T(8,128)(2,1)} %queue_ref.3, bf16[2048,256]{1,0:T(8,128)(2,1)} %bitcast.1), custom_call_target="tpu_custom_call" | custom-call | tf_op jit(solution)/shard_map/finish/pallas_call | solution.py:350

commit v8 on v7

--- a/solution.py
+++ b/solution.py
@@ -122,12 +122,9 @@
     def find(at):
         columns = [to_column(p_all[at + b].astype(F32), diag) for b in range(group)]
         target = jnp.concatenate(columns, axis=0).astype(jnp.int32) - i * key_dev
-        hits = lax.broadcasted_iota(jnp.int32, (rows, key_dev), 1) == target
-        row = jnp.dot(hits.astype(F32).astype(BF16), keys[...], preferred_element_type=F32)
-        return target, row
-
-    def work(at, found, start_stats):
-        target, row = found
+        return target
+
+    def work(at, target, start_stats):
         q = q_all[pl.ds(at, group)].reshape(rows, width)
         slab = keys[...]
         raw = lax.dot_general(q, slab, (((1,), (1,)), ((), ())), preferred_element_type=F32)
@@ -144,7 +141,9 @@
             stat_send[at + b, 2:3] = to_row(positive[span], diag) * scale
             stat_send[at + b, 3:4] = jnp.zeros((1, LANES), F32)
         start_stats()
-        part = jnp.dot(others, slab, preferred_element_type=F32)
+        stacked = jnp.concatenate([others, jnp.where(hits, 1.0, 0.0).astype(BF16)], axis=0)
+        both = jnp.dot(stacked, slab, preferred_element_type=F32)
+        part, row = both[:rows], both[rows:]
         high = part.astype(BF16)
         low = part - high.astype(F32)
         inside = jnp.logical_and(target >= 0, target < key_dev)

time: 22.7 us -> 22.7 us (level)
  no operation moved by 1% of the time
where the time goes in v8:
time: 22.7 us; the launch traced here: 22.6 us
  Pallas kernels  21.3 us (94%)
  between operations  1.29 us (6%)
    pallas_call x1, Pallas kernels, local(): pl.pallas_call(functools.partial(exchange, n, ngy, scale), out_shape=(jax...  19.2 us
    pallas_call x1, Pallas kernels, local(): pl.pallas_call(functools.partial(finish, n), out_shape=(jax.ShapeDtypeStr...  2.14 us

profile of v8, /device:TPU:0, one launch (start us, length us, event | category | flops | bytes accessed | tf_op | source)
XLA Modules:
  0.0 22.6 jit_solution(110536062406652903)
XLA Ops:
  1.3 19.2 %exchange.1 = (f32[1,128]{1,0:T(1,128)}, bf16[32,256]{1,0:T(8,128)(2,1)}, bf16[32,64,256]{2,1,0:T(8,128)(2,1)}) custom-call(bf16[32,256]{1,0:T(8,128)(2,1)} %q_ref.1, s32[32]{0:T(128)} %pos_ref.1, bf16[2048,256]{1,0:T(8,128)(2,1)} %queue_ref.3, bf16[64,256]{1,0:T(8,128)(2,1)} %nk_ref.1), custom_call_target="tpu_custom_call" | custom-call | flops 805306368 | bytes 2097152 | tf_op jit(solution)/shard_map/exchange/pallas_call | solution.py:310
  20.4 2.1 %finish.1 = (f32[32]{0:T(128)}, bf16[32,256]{1,0:T(8,128)(2,1)}, bf16[2048,256]{1,0:T(8,128)(2,1)}) custom-call(s32[1]{0:T(128)S(6)} %copy.8.step_ref, f32[1,128]{1,0:T(1,128)} %get-tuple-element.6.loss_ref, bf16[32,256]{1,0:T(8,128)(2,1)} %get-tuple-element.7.grad_ref, bf16[2048,256]{1,0:T(8,128)(2,1)} %queue_ref.3, bf16[2048,256]{1,0:T(8,128)(2,1)} %bitcast.1), custom_call_target="tpu_custom_call" | custom-call | tf_op jit(solution)/shard_map/finish/pallas_call | solution.py:349

commit v9 on v7

--- a/solution.py
+++ b/solution.py
@@ -116,7 +116,7 @@
     def go_on(z):
         same_core(lambda p: b_copy(p, z).start())
 
-    group = min(n, 256 // q_dev)
+    group = n // 2 if by_block else min(n, 256 // q_dev)
     rows = group * q_dev
 
     def find(at):
@@ -176,16 +176,25 @@
     keep(i).start()
     load_keys.wait()
     gx_peers(lambda p: wait_in(p_all.at[p], p_rs.at[p]))
-    whole = n == group
-    if whole:
-        found = find(0)
-    gx_peers(lambda p: wait_in(q_all.at[p], q_rs.at[p]))
-    if whole:
-        work(0, found, lambda: gx_peers(lambda p: s_copy(p).start()))
+    if by_block:
+        near = (i // group) * group
+        far = n - group - near
+        halves = (
+            (far, [far + b for b in range(group)]),
+            (near, [near + lax.rem(i - near + d, group) for d in range(1, group)]),
+        )
+        for at, peers in halves:
+            found = find(at)
+            for p in peers:
+                wait_in(q_all.at[p], q_rs.at[p])
+            work(at, found, lambda: [s_copy(p).start() for p in peers])
+            for p in peers:
+                g_copy(p).start()
     else:
+        gx_peers(lambda p: wait_in(q_all.at[p], q_rs.at[p]))
         pl.loop(0, n // group)(lambda c: work(c * group, find(c * group), lambda: None))
         gx_peers(lambda p: s_copy(p).start())
-    gx_peers(lambda p: g_copy(p).start())
+        gx_peers(lambda p: g_copy(p).start())
     part_recv[i] = part_send[i]
     stat_recv[i] = stat_send[i]
 

time: 22.7 us -> 22.7 us (level)
  no operation moved by 1% of the time
where the time goes in v9:
time: 22.7 us; the launch traced here: 22.5 us
  Pallas kernels  21.2 us (93%)
  between operations  1.29 us (6%)
    pallas_call x1, Pallas kernels, local(): pl.pallas_call(functools.partial(exchange, n, ngy, scale), out_shape=(jax...  19.1 us
    pallas_call x1, Pallas kernels, local(): pl.pallas_call(functools.partial(finish, n), out_shape=(jax.ShapeDtypeStr...  2.14 us

profile of v9, /device:TPU:0, one launch (start us, length us, event | category | flops | bytes accessed | tf_op | source)
XLA Modules:
  0.0 22.5 jit_solution(1590337814873080139)
XLA Ops:
  1.3 19.1 %exchange.1 = (f32[1,128]{1,0:T(1,128)}, bf16[32,256]{1,0:T(8,128)(2,1)}, bf16[32,64,256]{2,1,0:T(8,128)(2,1)}) custom-call(bf16[32,256]{1,0:T(8,128)(2,1)} %q_ref.1, s32[32]{0:T(128)} %pos_ref.1, bf16[2048,256]{1,0:T(8,128)(2,1)} %queue_ref.3, bf16[64,256]{1,0:T(8,128)(2,1)} %nk_ref.1), custom_call_target="tpu_custom_call" | custom-call | flops 805306368 | bytes 2097152 | tf_op jit(solution)/shard_map/exchange/pallas_call | solution.py:320
  20.4 2.1 %finish.1 = (f32[32]{0:T(128)}, bf16[32,256]{1,0:T(8,128)(2,1)}, bf16[2048,256]{1,0:T(8,128)(2,1)}) custom-call(s32[1]{0:T(128)S(6)} %copy.8.step_ref, f32[1,128]{1,0:T(1,128)} %get-tuple-element.6.loss_ref, bf16[32,256]{1,0:T(8,128)(2,1)} %get-tuple-element.7.grad_ref, bf16[2048,256]{1,0:T(8,128)(2,1)} %queue_ref.3, bf16[2048,256]{1,0:T(8,128)(2,1)} %bitcast.1), custom_call_target="tpu_custom_call" | custom-call | tf_op jit(solution)/shard_map/finish/pallas_call | solution.py:359
